TPU v7x, 128 devices: a whole 4x4x4 slice. The times are simulated.
128 devices in a mesh: gx: 16 (over z, x_lo, core), gy: 4 (over y), vert: 2 (over x_hi).
Axes of the slice: x: 4 (x_hi: 2, x_lo: 2; x = x_hi * 2 + x_lo), y: 4, z: 4, core: 2. Of those that a mesh axis runs over, the one named last changes fastest.
Arguments:
- vectors: bfloat16 [2, 3, 256, 16, 4096], P(None, None, 'vert', 'gx', 'gy'), may hold values from -6 to 6
- links: float32 [2, 2, 3, 3, 16, 4096], P(None, None, None, None, 'gx', 'gy'), may hold values from -4 to 4
- momenta: int32 [2, 3], replicated, may hold values from -2 to 2
- shifts_dir: int32 [3], replicated, may hold values from 0 to 2, each once
Outputs:
- elementals: float32 [256, 2, 3, 2, 256], P(('gx', 'gy'), None, None, None, 'vert')
Inputs may be any that keep to these rules, and one draw needn't show every extreme that they name: `momenta`: integer momentum components. `shifts_dir`: each of 0 (no displacement), 1 (one link along +x) and 2 (one link along +y) appears exactly once.
All inputs are finite; a program needn't handle non-finite values.
Results may differ from a plain program's by a relative error of at most 0.0029.
Values may be sent and summed in bfloat16 or wider, within the bound.
A program may use at most 128 MiB of HBM per device.

v0:
```python
import math

import jax
import jax.numpy as jnp
from jax import lax
from jax.sharding import PartitionSpec as P

NZ = 64


def passed_along(block, axis, distance):
    devices = range(lax.axis_size(axis))
    route = [((i - distance) % len(devices), i) for i in devices]
    return lax.ppermute(block, axis, route)


def phase_tables(mom, xpos, ypos, zpos, nx, ny, nz):
    frac_x = jnp.mod(mom[0] * xpos, nx).astype(jnp.float32) / nx
    frac_y = jnp.mod(mom[1] * ypos, ny).astype(jnp.float32) / ny
    frac_z = jnp.mod(mom[2] * zpos, nz).astype(jnp.float32) / nz
    rest = (frac_y[:, None] + frac_z[None, :]).reshape(-1)
    angle = 2.0 * math.pi * (frac_x[:, None] + rest[None, :])
    return (jnp.cos(angle), jnp.sin(angle))


def transport(link, field):
    fre = field[0].astype(jnp.float32)
    fim = field[1].astype(jnp.float32)
    out_re = []
    out_im = []
    for row in range(3):
        acc_re = 0.0
        acc_im = 0.0
        for col in range(3):
            lre = link[0, row, col][None]
            lim = link[1, row, col][None]
            acc_re = acc_re + lre * fre[col] - lim * fim[col]
            acc_im = acc_im + lre * fim[col] + lim * fre[col]
        out_re.append(acc_re)
        out_im.append(acc_im)
    return (jnp.stack(out_re, axis=0), jnp.stack(out_im, axis=0))


def pair_operand(uvr, uvi, cosine, sine):
    wre = (uvr * cosine + uvi * sine).astype(jnp.bfloat16)
    wim = (uvi * cosine - uvr * sine).astype(jnp.bfloat16)
    return (wre, wim)


def row_terms(piece, wre, wim, nmom, ndisp, scale):
    count = piece.shape[2]
    left = piece.reshape(2, 3, count, -1)

    def prod(a, b):
        return jnp.einsum("cas,pcbs->apb", a, b, preferred_element_type=jnp.float32)

    ere = prod(left[0], wre) + prod(left[1], wim)
    eim = prod(left[0], wim) - prod(left[1], wre)
    both = jnp.stack([ere, eim], axis=2)
    return both.reshape(count, nmom, ndisp, 2, wre.shape[2]) * scale


def shift_x(field):
    x_recv = passed_along(field, "gx", -1)
    return jnp.concatenate([field[:, :, :, 1:, :], x_recv], axis=3)


def operands(field, ahead, upward, link_part, momenta, shifts_dir, xpos, ypos, nx, ny):
    count = field.shape[2]
    nmom = momenta.shape[0]
    ndisp = shifts_dir.shape[0]
    zpos = jnp.arange(NZ, dtype=jnp.int32)
    tables = [phase_tables(momenta[m], xpos, ypos, zpos, nx, ny, NZ) for m in range(nmom)]
    fields = [
        lax.switch(
            shifts_dir[k],
            [
                lambda: (field[0].astype(jnp.float32), field[1].astype(jnp.float32)),
                lambda: transport(link_part[0], ahead),
                lambda: transport(link_part[1], upward),
            ],
        )
        for k in range(ndisp)
    ]
    real_parts = []
    imag_parts = []
    for m in range(nmom):
        for k in range(ndisp):
            wre, wim = pair_operand(fields[k][0], fields[k][1], tables[m][0], tables[m][1])
            real_parts.append(wre.reshape(3, count, -1))
            imag_parts.append(wim.reshape(3, count, -1))
    return (jnp.stack(real_parts, axis=0), jnp.stack(imag_parts, axis=0))


def per_device(vectors, links, momenta, shifts_dir):
    sx = vectors.shape[3]
    syz = vectors.shape[4]
    sy = syz // NZ
    nx = sx * lax.axis_size("gx")
    ny = sy * lax.axis_size("gy")
    nmom = momenta.shape[0]
    ndisp = shifts_dir.shape[0]
    scale = 1.0 / math.sqrt(3.0 * nx * ny * NZ)
    xpos = lax.axis_index("gx") * sx + jnp.arange(sx, dtype=jnp.int32)
    ahead = shift_x(vectors)
    y_recv = passed_along(vectors[:, :, :, :, 0:NZ], "gy", -1)
    upward = jnp.concatenate([vectors[:, :, :, :, NZ:], y_recv], axis=4)
    ypos = lax.axis_index("gy") * sy + jnp.arange(sy, dtype=jnp.int32)
    wre_all, wim_all = operands(
        vectors, ahead, upward, links, momenta, shifts_dir, xpos, ypos, nx, ny
    )
    terms = row_terms(
        lax.all_gather(vectors, "vert", axis=2, tiled=True), wre_all, wim_all, nmom, ndisp, scale
    )
    return lax.psum_scatter(terms, ("gx", "gy"), scatter_dimension=0, tiled=True)


def solution(mesh):
    in_specs = (P(None, None, "vert", "gx", "gy"), P(None, None, None, None, "gx", "gy"), P(), P())
    out_specs = P(("gx", "gy"), None, None, None, "vert")
    return jax.shard_map(
        per_device, mesh=mesh, in_specs=in_specs, out_specs=out_specs, check_vma=False
    )
```

profile of v0, /device:TPU:0, one launch (start us, length us, event | category | flops | bytes accessed | tf_op | source)
XLA Modules:
  0.0 649.3 jit_solution(10121162028650612692)
XLA Ops:
  6.5 4.5 collective-permute-start
  12.0 3.1 collective-permute-start.1
  16.6 1.9 slice.854
  24.7 1.8 pad_maximum_fusion.12
  26.5 15.2 %collective-permute-done = bf16[2,3,128,1,1024]{4,2,3,1,0:T(8,128)(2,1)} collective-permute-done((bf16[2,3,128,1,1024]{4,2,3,1,0:T(8,128)(2,1)}, bf16[2,3,128,1,1024]{4,2,3,1,0:T(8,128)(2,1)}, u32[]{:S(2)}, u32[]{:S(2)}) %collective-permute-start) | collective-permute-done | bytes 1572896 | tf_op jit(solution)/shard_map/ppermute | solution.py:14
  41.7 4.9 conditional.3
  41.8 1.8 slice_convert_fusion
  44.7 1.9 pad_maximum_fusion
  46.6 2.0 conditional.4
  46.6 2.0 bitcast_convert_fusion.2
  48.6 3.0 conditional.5
  51.7 3.7 fusion.37
  55.3 1.7 fusion.45
  57.0 1.6 fusion.53
  59.5 1.7 fusion.35
  61.2 1.7 fusion.43
  62.9 1.7 fusion.51
  64.6 1.7 all-gather.2.cloned.1.call-done
  66.3 4.4 fusion.28
  70.7 3.8 fusion.33
  75.4 4.4 fusion.29
  79.8 3.8 fusion.32
  84.5 2.8 maximum_multiply_fusion
  89.2 552.0 %all-reduce.3.cloned.1.call-done = f32[256,2,3,2,128]{4,3,2,1,0:T(2,128)} async-done(((f32[256,2,3,2,128]{4,3,2,1,0:T(2,128)}), f32[256,2,3,2,128]{4,3,2,1,0:T(2,128)}) %all-reduce.3.cloned.1.call-update) | async-done | bytes 1572880
  (57 shorter events, 14.8 us)
Async XLA Ops:
  6.5 10.0 %copy-start = (bf16[2,3,128,1,1024]{4,2,3,1,0:T(8,128)(2,1)S(1)}, bf16[2,3,128,1,1024]{4,2,3,1,0:T(8,128)(2,1)}, u32[]{:S(2)}) copy-start(bf16[2,3,128,1,1024]{4,2,3,1,0:T(8,128)(2,1)} %param.13) | copy-start | bytes 4718596
  6.5 8.6 %copy-start.7 = (s32[2,3]{1,0:T(2,128)S(1)}, s32[2,3]{1,0:T(2,128)}, u32[]{:S(2)}) copy-start(s32[2,3]{1,0:T(2,128)} %param.15) | copy-start | bytes 76
  6.5 59.8 %all-gather.2.cloned.1.call-start = ((), (), s32[]{:S(2)}) async-start(), calls=%async_computation | async-start | bytes 4718592 | tf_op jit(solution)/shard_map/all_gather | solution.py:113
  6.5 35.2 %collective-permute-start = (bf16[2,3,128,1,1024]{4,2,3,1,0:T(8,128)(2,1)}, bf16[2,3,128,1,1024]{4,2,3,1,0:T(8,128)(2,1)}, u32[]{:S(2)}, u32[]{:S(2)}) collective-permute-start(bf16[2,3,128,1,1024]{4,2,3,1,0:T(8,128)(2,1)} %param.13), channel_id=1, source_target_pairs={{8,0},{16,8},{24,16},{32,24},{40,32},{48,40},{56,48},{64,56},{72,6... | collective-permute-start | bytes 4718600 | tf_op jit(solution)/shard_map/ppermute | solution.py:14
  12.0 12.7 %collective-permute-start.1 = (bf16[2,3,128,1,64]{4,2,3,1,0:T(8,128)(2,1)S(1)}, bf16[2,3,128,1,64]{4,2,3,1,0:T(8,128)(2,1)S(1)}, u32[]{:S(2)}, u32[]{:S(2)}) collective-permute-start(bf16[2,3,128,1,64]{4,2,3,1,0:T(8,128)(2,1)S(1)} %slice.855), channel_id=1, source_target_pairs={{2,0},{4,2},{6,4},{0,6},{3,1},{5,3},{7,5},{1,7},{10,8},{12,10},{14... | collective-permute-start | bytes 294920 | tf_op jit(solution)/shard_map/ppermute | solution.py:14
  15.1 626.0 %all-reduce.3.cloned.1.call-start = ((), (), s32[]{:S(2)}) async-start(), calls=%async_computation.1 | async-start | bytes 3145728
  16.6 5.6 copy-start.8
  24.7 17.1 %copy-start.6 = (f32[2,2,3,3,1,1024]{5,4,3,2,1,0:T(1,128)S(1)}, f32[2,2,3,3,1,1024]{5,4,3,2,1,0:T(1,128)}, u32[]{:S(2)}) copy-start(f32[2,2,3,3,1,1024]{5,4,3,2,1,0:T(1,128)} %param.14) | copy-start | bytes 442372
  51.7 3.7 copy-start.3
  51.7 3.7 copy-start.4
  55.3 1.7 copy-start.5
  57.0 1.6 copy-start.1
  57.0 2.4 copy-start.2
  66.3 4.4 copy-start.9
  75.4 4.4 copy-start.10
  87.3 0.7 copy-start.11
Sparse Core Ops, SparseCore 0:
  15.2 51.0 all-gather.1
  87.4 553.6 all-reduce.2
where the time goes:
time: 650 us; the launch traced here: 649 us
  waiting for transfers between devices  569 us (88%)
  other arithmetic  29.2 us (4%)
  between operations  17.4 us (3%)
  matrix products  16.3 us (3%)
  local copies, waits for them, and re-layouts  9.74 us (1%)
  starting transfers between devices  7.61 us (1%)
    unnamed x3, waiting for transfers between devices  552 us
    dot_general x4, matrix products, prod(): return jnp.einsum('cas,pcbs->apb', a, b, preferred_element_type=jnp.float32)  16.3 us
    ppermute x2, waiting for transfers between devices, passed_along(): return lax.ppermute(block, axis, route)  15.2 us
  transfers between devices with their start and end apart: 4, of which 3 were waited for; matrix products, arithmetic and copies ran while one was open for 5% of the time, Pallas kernels for 0%

commit v1 on v0

v1 whole, which is shorter than its diff:
```python
import math

import jax
import jax.numpy as jnp
from jax import lax
from jax.experimental import pallas as pl
from jax.experimental.pallas import tpu as pltpu
from jax.sharding import PartitionSpec as P

MESH = pl.DeviceIdType.MESH
F32 = jnp.float32
BF16 = jnp.bfloat16

NSUB = 2
U = 128 // NSUB
NT = (((1,), (1,)), ((), ()))
SCALE = 1.0 / math.sqrt(3.0 * 16 * 64 * 64)
PEERS_X = [(d, dc) for d in (2, 1, 3, 0) for dc in (0, 1) if d or dc]


def kernel(
    vec_hbm, links_hbm, mom_ref, dir_ref, out_ref,
    vbuf, lbuf, perm, sbuf, lhs, neg, xh, hs, hr, lsend, ul, ct, st, wt,
    ek, ex, er, sz, rz, sx, rx, oz, ox, sz2, rz2, sx2, rx2, sy, ry, fin,
    vsem, lsem, a_s, a_r, l_s, l_r, xh_s, xh_r, yh_s, yh_r, c_s, c_r,
    z1_s, z1_r, x1_s, x1_r, z2_s, z2_r, x2_s, x2_r, y3_s, y3_r,
):
    gx, gy, hi = lax.axis_index("gx"), lax.axis_index("gy"), lax.axis_index("vert")
    z, lo, c = gx // 4, (gx // 2) % 2, gx % 2
    x = hi * 2 + lo
    e = x * 2 + c
    layer = lo * 2 + c

    def dev(dz=0, dy=0, dx=0, dc=0):
        tx = (x + dx) % 4
        tz = (z + dz) % 4
        tc = (c + dc) % 2
        return (tz * 4 + (tx % 2) * 2 + tc, (gy + dy) % 4, tx // 2)

    def remote(src, dst, s, r, where):
        return pltpu.make_async_remote_copy(
            src_ref=src, dst_ref=dst, send_sem=s, recv_sem=r, device_id=where, device_id_type=MESH
        )

    loads = []
    for u in range(NSUB):
        cp = pltpu.make_async_copy(
            vec_hbm.at[:, pl.ds(u * U, U), :], vbuf.at[:, pl.ds(u * U, U), :], vsem.at[u]
        )
        cp.start()
        loads.append(cp)
    lcopy = pltpu.make_async_copy(links_hbm, lbuf, lsem)
    lcopy.start()

    barrier = pltpu.get_barrier_semaphore()
    peers = [dev(dx=d, dc=dc) for d, dc in PEERS_X]
    peers += [dev(dz=d) for d in (1, 2, 3)] + [dev(dy=d) for d in (1, 2, 3)]
    for p in peers:
        pl.semaphore_signal(barrier, inc=1, device_id=p, device_id_type=MESH)

    site = lax.broadcasted_iota(jnp.int32, (1024, 256), 0)
    col = lax.broadcasted_iota(jnp.int32, (1024, 256), 1)
    core_of = jnp.where(col < 128, c, 1 - c)
    lane = col % 128
    want = (lane // 8) * 64 + lane % 8 + core_of * 8
    for d in range(4):
        q = (x + d) % 4
        perm[d] = jnp.where(site == want + q * 16, 1.0, 0.0).astype(BF16)

    row = lax.broadcasted_iota(jnp.int32, (8, 128), 0)
    ln = lax.broadcasted_iota(jnp.int32, (8, 128), 1)
    first = row < 4
    px = jnp.where(first, mom_ref[0, 0], mom_ref[1, 0])
    py = jnp.where(first, mom_ref[0, 1], mom_ref[1, 1])
    pz = jnp.where(first, mom_ref[0, 2], mom_ref[1, 2])
    turn = (
        4 * ((px * (z * 4 + row % 4)) & 15)
        + ((py * (gy * 16 + ln // 8)) & 63)
        + ((pz * (e * 8 + ln % 8)) & 63)
    )
    angle = (2.0 * math.pi) * (turn.astype(F32) * (1.0 / 64.0))
    ct[...] = jnp.cos(angle)
    st[...] = jnp.sin(angle)

    pl.semaphore_wait(barrier, len(peers))

    def a2a(u, d, dc):
        return remote(
            sbuf.at[d * 2 + dc, :, pl.ds(u * U, U), :],
            lhs.at[pl.ds(layer * 6, 6), hi, pl.ds(u * U, U), :],
            a_s.at[u, d * 2 + dc], a_r.at[u, d * 2 + dc], dev(dx=d, dc=dc),
        )

    def a2a_in(u, d, dc):
        sx_ = (x - d + 4) % 4
        slayer = (sx_ % 2) * 2 + (c + dc) % 2
        return remote(
            sbuf.at[d * 2 + dc, :, pl.ds(u * U, U), :],
            lhs.at[pl.ds(slayer * 6, 6), sx_ // 2, pl.ds(u * U, U), :],
            a_s.at[u, d * 2 + dc], a_r.at[u, d * 2 + dc], dev(dx=d, dc=dc),
        )

    for u in range(NSUB):
        loads[u].wait()
        mine = vbuf[:, u * U:(u + 1) * U, :].reshape(6 * U, 1024)
        for d in (2, 1, 3, 0):
            moved = jnp.dot(mine, perm[d], preferred_element_type=F32).astype(BF16)
            for dc in (0, 1):
                part = moved[:, dc * 128:(dc + 1) * 128].reshape(6, U, 128)
                if d or dc:
                    sbuf[d * 2 + dc, :, u * U:(u + 1) * U, :] = part
                    a2a(u, d, dc).start()
                else:
                    lhs[pl.ds(layer * 6, 6), hi, u * U:(u + 1) * U, :] = part
        if u == 0:
            lcopy.wait()
            rows = [lbuf[pl.ds(t, 36, stride=8), :] for t in range(8)]
            link = jnp.concatenate(rows, axis=1)
            link = jnp.concatenate([link, jnp.zeros((12, 1024), F32)], axis=0)
            part0 = link.astype(BF16)
            rest = link - part0.astype(F32)
            part1 = rest.astype(BF16)
            part2 = (rest - part1.astype(F32)).astype(BF16)
            parts = jnp.concatenate([part0, part1, part2], axis=0)
            for i in range(2):
                slot = 0 if i == 0 else 1 + 2 * lo
                got = jnp.dot(parts, perm[slot], preferred_element_type=F32)
                total = (got[0:48] + got[48:96]) + got[96:144]
                for dc in (0, 1):
                    piece = total[:, dc * 128:(dc + 1) * 128]
                    if i or dc:
                        lsend[i * 2 + dc] = piece
                    else:
                        ul[layer] = piece

    def link_copy(i, dc, slayer):
        tx = hi * 2 + (lo + i) % 2
        return remote(
            lsend.at[i * 2 + dc], ul.at[slayer], l_s.at[i * 2 + dc], l_r.at[i * 2 + dc],
            (z * 4 + (tx % 2) * 2 + (c + dc) % 2, gy, hi),
        )

    LINKS = [(0, 1), (1, 0), (1, 1)]
    for i, dc in LINKS:
        link_copy(i, dc, layer).start()
    for i, dc in LINKS:
        link_copy(i, dc, ((lo + i) % 2) * 2 + (c + dc) % 2).wait_recv()

    lane16 = lax.broadcasted_iota(jnp.int32, (16, 128), 1)

    def transport(l, d, f):
        out = []
        for r in range(3):
            are = aim = None
            for k in range(3):
                ure = ul[l, pl.ds(((d * 2 + 0) * 3 + r) * 3 + k, 1), :]
                uim = ul[l, pl.ds(((d * 2 + 1) * 3 + r) * 3 + k, 1), :]
                tre = ure * f[k] - uim * f[3 + k]
                tim = ure * f[3 + k] + uim * f[k]
                are = tre if are is None else are + tre
                aim = tim if aim is None else aim + tim
            out.append((are, aim))
        return out

    def put(l, d, v, rows, f):
        for m in range(2):
            cs = ct[pl.ds(m * 4 + l, 1), :]
            sn = st[pl.ds(m * 4 + l, 1), :]
            for r in range(3):
                fre, fim = f[r]
                wre = (fre * cs + fim * sn).astype(BF16)
                wim = (fim * cs - fre * sn).astype(BF16)
                wt[m * 3 + d, v, rows, pl.ds((l * 6 + r) * 128, 128)] = wre
                wt[m * 3 + d, v, rows, pl.ds((l * 6 + 3 + r) * 128, 128)] = wim

    def xh_copy(u):
        return remote(
            lhs.at[pl.ds(0, 6), :, pl.ds(u * U, U), :], xh.at[:, :, pl.ds(u * U, U), :],
            xh_s.at[u], xh_r.at[u], dev(dz=3),
        )

    def yh_copy(u):
        return remote(
            hs.at[:, pl.ds(u * U, U), :], hr.at[:, pl.ds(u * U, U), :],
            yh_s.at[u], yh_r.at[u], dev(dy=3),
        )

    CH = U // 16
    for u in range(NSUB):
        for d, dc in PEERS_X:
            a2a_in(u, d, dc).wait_recv()
        xh_copy(u).start()

        def pack(j, carry):
            rows = pl.ds(pl.multiple_of(u * U + j * 16, 16), 16)
            for i in range(6):
                acc = lhs[i, 0, rows, :].astype(F32)
                for s in range(1, 8):
                    v, l = s // 4, s % 4
                    piece = pltpu.roll(lhs[l * 6 + i, v, rows, :].astype(F32), 8 * s, 1)
                    acc = jnp.where(lane16 < 8 * s, acc, piece)
                hs[i, rows, :] = acc.astype(BF16)
            for l in range(4):
                for r in range(3):
                    for v in range(2):
                        neg[l * 3 + r, v, rows, :] = -lhs[l * 6 + 3 + r, v, rows, :]
            return carry

        lax.fori_loop(0, CH, pack, 0)
        yh_copy(u).start()

        def free(j, carry):
            v = j // CH
            rows = pl.ds(pl.multiple_of(u * U + (j % CH) * 16, 16), 16)
            for l in range(4):
                f = [lhs[l * 6 + i, v, rows, :].astype(F32) for i in range(6)]
                put(l, 0, v, rows, [(f[r], f[3 + r]) for r in range(3)])
                if l < 3:
                    f = [lhs[l * 6 + 6 + i, v, rows, :].astype(F32) for i in range(6)]
                    put(l, 1, v, rows, transport(l, 0, f))
            return carry

        lax.fori_loop(0, 2 * CH, free, 0)
        xh_copy(u).wait_recv()
        yh_copy(u).wait_recv()

        def halo(j, carry):
            v = j // CH
            rows = pl.ds(pl.multiple_of(u * U + (j % CH) * 16, 16), 16)
            f = [xh[i, v, rows, :].astype(F32) for i in range(6)]
            put(3, 1, v, rows, transport(3, 0, f))
            for l in range(4):
                f = []
                for i in range(6):
                    here = pltpu.roll(lhs[l * 6 + i, v, rows, :].astype(F32), 120, 1)
                    shift = (248 - 8 * (v * 4 + l)) % 128
                    edge = pltpu.roll(hr[i, rows, :].astype(F32), shift, 1)
                    f.append(jnp.where(lane16 < 120, here, edge))
                put(l, 2, v, rows, transport(l, 1, f))
            return carry

        lax.fori_loop(0, 2 * CH, halo, 0)

    def core_copy(mk):
        return remote(ex.at[mk], er.at[mk], c_s.at[mk], c_r.at[mk], dev(dc=1))

    def products(mk, carry):
        right = wt[mk].reshape(256, 3072)
        re = [lhs[t].reshape(256, 128) for t in range(24)]
        im = []
        for l in range(4):
            im += [neg[l * 3 + r].reshape(256, 128) for r in range(3)]
            im += [lhs[l * 6 + r].reshape(256, 128) for r in range(3)]
        for part, tiles in enumerate((re, im)):
            left = jnp.concatenate(tiles, axis=1)
            prod = lax.dot_general(left, right, NT, preferred_element_type=F32)
            groups = prod.reshape(8, 2, 16, 256)
            even, odd = groups[:, 0], groups[:, 1]
            ek[mk, part] = jnp.where(c == 0, even, odd)
            ex[mk, part] = jnp.where(c == 0, odd, even).astype(BF16)
        core_copy(mk).start()
        return carry

    lax.fori_loop(0, 6, products, 0)

    for mk in range(6):
        core_copy(mk).wait_recv()
        k = mk % 3
        for part in range(2):
            total = ek[mk, part] + er[mk, part].astype(F32)
            if mk < 3:
                ek[mk, part] = total
                for t in range(4):
                    sz[t, k, part] = total[2 * t:2 * t + 2].astype(BF16)
            else:
                ek[mk, part] = total
                four = total.reshape(4, 2, 16, 256)
                for t in range(4):
                    half = four[:, t % 2][:, :, (t // 2) * 128:(t // 2) * 128 + 128]
                    sx[t, k, part] = half.astype(BF16)

    def z1(d):
        return remote(sz.at[(z + d) % 4], rz.at[d - 1], z1_s.at[d - 1], z1_r.at[d - 1], dev(dz=d))

    def x1(d):
        return remote(sx.at[(x + d) % 4], rx.at[d - 1], x1_s.at[d - 1], x1_r.at[d - 1], dev(dx=d))

    for d in (2, 1, 3):
        z1(d).start()
        x1(d).start()
    for d in (1, 3, 2):
        z1(d).wait_recv()
        x1(d).wait_recv()
    for k in range(3):
        for part in range(2):
            total = ek[k, part, pl.ds(z * 2, 2)]
            for d in range(3):
                total = total + rz[d, k, part].astype(F32)
            for t in range(4):
                sx2[t, k, part] = total[t % 2, :, (t // 2) * 128:(t // 2) * 128 + 128]
            lo_part = [ek[3 + k, part, t * 2 + lo, :, pl.ds(pl.multiple_of(hi * 128, 128), 128)] for t in range(4)]
            for t in range(4):
                total = lo_part[t]
                for d in range(3):
                    total = total + rx[d, k, part, t].astype(F32)
                sz2[t, k, part] = total

    def z2(d):
        return remote(sz2.at[(z + d) % 4], rz2.at[d - 1], z2_s.at[d - 1], z2_r.at[d - 1], dev(dz=d))

    def x2(d):
        return remote(sx2.at[(x + d) % 4], rx2.at[d - 1], x2_s.at[d - 1], x2_r.at[d - 1], dev(dx=d))

    for d in (2, 1, 3):
        z2(d).start()
        x2(d).start()
    for d in (1, 3, 2):
        z2(d).wait_recv()
        x2(d).wait_recv()
    for k in range(3):
        for part in range(2):
            one = sx2[x, k, part]
            two = sz2[z, k, part]
            for d in range(3):
                one = one + rx2[d, k, part]
                two = two + rz2[d, k, part]
            for m, total in enumerate((one, two)):
                j = (m * 3 + k) * 2 + part
                for t in range(4):
                    sy[t, pl.ds(j * 4, 4), :] = total[t * 4:t * 4 + 4]

    def y3(d):
        return remote(sy.at[(gy + d) % 4], ry.at[d - 1], y3_s.at[d - 1], y3_r.at[d - 1], dev(dy=d))

    for d in (2, 1, 3):
        y3(d).start()
    for d in (1, 3, 2):
        y3(d).wait_recv()
    fin[...] = (((sy[gy] + ry[0]) + ry[1]) + ry[2]) * SCALE
    for m in range(2):
        for part in range(2):
            by_dir = [fin[pl.ds(((m * 3 + d) * 2 + part) * 4, 4), :] for d in range(3)]
            for k in range(3):
                want_dir = dir_ref[k]
                val = jnp.where(want_dir == 0, by_dir[0], jnp.where(want_dir == 1, by_dir[1], by_dir[2]))
                out_ref[pl.ds((m * 3 + k) * 2 + part, 4, stride=12), :] = val

    for u in range(NSUB):
        for d, dc in PEERS_X:
            a2a(u, d, dc).wait_send()
        xh_copy(u).wait_send()
        yh_copy(u).wait_send()
    for i, dc in LINKS:
        link_copy(i, dc, layer).wait_send()
    for mk in range(6):
        core_copy(mk).wait_send()
    for d in (1, 2, 3):
        z1(d).wait_send()
        x1(d).wait_send()
        z2(d).wait_send()
        x2(d).wait_send()
        y3(d).wait_send()


def per_device(vectors, links, momenta, shifts_dir):
    dma = lambda *n: pltpu.SemaphoreType.DMA(n)
    vm = pltpu.VMEM
    out = pl.pallas_call(
        kernel,
        out_shape=jax.ShapeDtypeStruct((48, 128), F32),
        in_specs=[
            pl.BlockSpec(memory_space=pl.ANY),
            pl.BlockSpec(memory_space=pl.ANY),
            pl.BlockSpec(memory_space=pltpu.SMEM),
            pl.BlockSpec(memory_space=pltpu.SMEM),
        ],
        out_specs=pl.BlockSpec(memory_space=pltpu.VMEM),
        scratch_shapes=[
            vm((6, 128, 1024), BF16),
            vm((288, 128), F32),
            vm((4, 1024, 256), BF16),
            vm((8, 6, 128, 128), BF16),
            vm((24, 2, 128, 128), BF16),
            vm((12, 2, 128, 128), BF16),
            vm((6, 2, 128, 128), BF16),
            vm((6, 128, 128), BF16),
            vm((6, 128, 128), BF16),
            vm((4, 48, 128), F32),
            vm((4, 48, 128), F32),
            vm((8, 128), F32),
            vm((8, 128), F32),
            vm((6, 2, 128, 3072), BF16),
            vm((6, 2, 8, 16, 256), F32),
            vm((6, 2, 8, 16, 256), BF16),
            vm((6, 2, 8, 16, 256), BF16),
            vm((4, 3, 2, 2, 16, 256), BF16),
            vm((3, 3, 2, 2, 16, 256), BF16),
            vm((4, 3, 2, 4, 16, 128), BF16),
            vm((3, 3, 2, 4, 16, 128), BF16),
            vm((8, 128), F32),
            vm((8, 128), F32),
            vm((4, 3, 2, 16, 128), F32),
            vm((3, 3, 2, 16, 128), F32),
            vm((4, 3, 2, 16, 128), F32),
            vm((3, 3, 2, 16, 128), F32),
            vm((4, 48, 128), F32),
            vm((3, 48, 128), F32),
            vm((48, 128), F32),
            dma(NSUB), pltpu.SemaphoreType.DMA,
            dma(NSUB, 8), dma(NSUB, 8), dma(4), dma(4),
            dma(NSUB), dma(NSUB), dma(NSUB), dma(NSUB), dma(6), dma(6),
            dma(3), dma(3), dma(3), dma(3), dma(3), dma(3), dma(3), dma(3), dma(3), dma(3),
        ],
        compiler_params=pltpu.CompilerParams(
            collective_id=0, has_side_effects=True, vmem_limit_bytes=56 * 1024 * 1024
        ),
        name="elementals",
    )(vectors.reshape(6, 128, 1024), links.reshape(288, 128), momenta, shifts_dir)
    return out.reshape(4, 2, 3, 2, 128)


def solution(mesh):
    in_specs = (P(None, None, "vert", "gx", "gy"), P(None, None, None, None, "gx", "gy"), P(), P())
    out_specs = P(("gx", "gy"), None, None, None, "vert")
    return jax.shard_map(
        per_device, mesh=mesh, in_specs=in_specs, out_specs=out_specs, check_vma=False
    )
```

time: 650 us -> 68.4 us (0.11)
  waiting for transfers between devices: 569 us -> 0 us
  Pallas kernels: 0 us -> 66.8 us
  other arithmetic: 29.2 us -> 0 us
  between operations: 17.4 us -> 0.01 us
  matrix products: 16.3 us -> 0 us
  local copies, waits for them, and re-layouts: 9.74 us -> 1.35 us
  starting transfers between devices: 7.61 us -> 0 us
    unnamed x3 -> x0, waiting for transfers between devices: 552 us -> none
    pallas_call x0 -> x1, Pallas kernels: none -> 66.8 us  [per_device(): pl.pallas_call(kernel, out_shape=jax.ShapeDtypeStruct((48, 128), F32), in...]
    dot_general x4 -> x0, matrix products: 16.3 us -> none  [prod(): return jnp.einsum('cas,pcbs->apb', a, b, preferred_element_type=jnp.float32)]
    ppermute x2 -> x0, waiting for transfers between devices: 15.2 us -> none  [passed_along(): return lax.ppermute(block, axis, route)]
    unnamed x5 -> x0, other arithmetic: 10.4 us -> none
    ppermute x2 -> x0, starting transfers between devices: 7.57 us -> none  [passed_along(): return lax.ppermute(block, axis, route)]
  transfers between devices with their start and end apart: 4 -> 0, of which waited for: 3 -> 0; matrix products, arithmetic and copies ran while one was open for 5% -> 0% of each run, Pallas kernels for 0% -> 0%
where the time goes in v1:
time: 68.4 us; the launch traced here: 68.2 us
  Pallas kernels  66.8 us (98%)
  local copies, waits for them, and re-layouts  1.35 us (2%)
    pallas_call x1, Pallas kernels, per_device(): pl.pallas_call(kernel, out_shape=jax.ShapeDtypeStruct((48, 128), F32), in...  66.8 us

profile of v1, /device:TPU:0, one launch (start us, length us, event | category | flops | bytes accessed | tf_op | source)
XLA Modules:
  0.0 68.2 jit_solution(12374963712046524180)
XLA Ops:
  0.0 66.8 %elementals.1 = f32[48,128]{1,0:T(8,128)} custom-call(bf16[6,128,1024]{2,1,0:T(8,128)(2,1)} %bitcast.3, f32[288,128]{1,0:T(8,128)} %bitcast.4, s32[2,3]{1,0:T(2,128)} %mom_ref.1, s32[3]{0:T(128)} %dir_ref.1), custom_call_target="tpu_custom_call" | custom-call | tf_op jit(solution)/shard_map/elementals/pallas_call | solution.py:368
  66.8 1.4 %copy.6 = f32[4,2,3,2,128]{4,3,2,1,0:T(2,128)} copy(f32[4,2,3,2,128]{4,3,2,1,0:T(2,128)} %bitcast.5) | data formatting | bytes 49152

commit v2 on v1

--- a/solution.py
+++ b/solution.py
@@ -11,7 +11,9 @@
 F32 = jnp.float32
 BF16 = jnp.bfloat16
 
-NSUB = 2
+NSUB = 4
+AHEAD = 2
+POINTS = (2, 3)
 U = 128 // NSUB
 NT = (((1,), (1,)), ((), ()))
 SCALE = 1.0 / math.sqrt(3.0 * 16 * 64 * 64)
@@ -21,7 +23,7 @@
 def kernel(
     vec_hbm, links_hbm, mom_ref, dir_ref, out_ref,
     vbuf, lbuf, perm, sbuf, lhs, neg, xh, hs, hr, lsend, ul, ct, st, wt,
-    ek, ex, er, sz, rz, sx, rx, oz, ox, sz2, rz2, sx2, rx2, sy, ry, fin,
+    ek, ex, er, sz, rz, sx, rx, sz2, rz2, sx2, rx2, sy, ry, fin,
     vsem, lsem, a_s, a_r, l_s, l_r, xh_s, xh_r, yh_s, yh_r, c_s, c_r,
     z1_s, z1_r, x1_s, x1_r, z2_s, z2_r, x2_s, x2_r, y3_s, y3_r,
 ):
@@ -36,6 +38,16 @@
         tz = (z + dz) % 4
         tc = (c + dc) % 2
         return (tz * 4 + (tx % 2) * 2 + tc, (gy + dy) % 4, tx // 2)
+
+    pending = []
+
+    def go(copy):
+        copy.start()
+        pending.append(copy)
+
+    def finish():
+        for copy in pending:
+            copy.wait_send()
 
     def remote(src, dst, s, r, where):
         return pltpu.make_async_remote_copy(
@@ -100,7 +112,7 @@
             a_s.at[u, d * 2 + dc], a_r.at[u, d * 2 + dc], dev(dx=d, dc=dc),
         )
 
-    for u in range(NSUB):
+    def move(u):
         loads[u].wait()
         mine = vbuf[:, u * U:(u + 1) * U, :].reshape(6 * U, 1024)
         for d in (2, 1, 3, 0):
@@ -109,29 +121,10 @@
                 part = moved[:, dc * 128:(dc + 1) * 128].reshape(6, U, 128)
                 if d or dc:
                     sbuf[d * 2 + dc, :, u * U:(u + 1) * U, :] = part
-                    a2a(u, d, dc).start()
                 else:
                     lhs[pl.ds(layer * 6, 6), hi, u * U:(u + 1) * U, :] = part
-        if u == 0:
-            lcopy.wait()
-            rows = [lbuf[pl.ds(t, 36, stride=8), :] for t in range(8)]
-            link = jnp.concatenate(rows, axis=1)
-            link = jnp.concatenate([link, jnp.zeros((12, 1024), F32)], axis=0)
-            part0 = link.astype(BF16)
-            rest = link - part0.astype(F32)
-            part1 = rest.astype(BF16)
-            part2 = (rest - part1.astype(F32)).astype(BF16)
-            parts = jnp.concatenate([part0, part1, part2], axis=0)
-            for i in range(2):
-                slot = 0 if i == 0 else 1 + 2 * lo
-                got = jnp.dot(parts, perm[slot], preferred_element_type=F32)
-                total = (got[0:48] + got[48:96]) + got[96:144]
-                for dc in (0, 1):
-                    piece = total[:, dc * 128:(dc + 1) * 128]
-                    if i or dc:
-                        lsend[i * 2 + dc] = piece
-                    else:
-                        ul[layer] = piece
+                if u < AHEAD and (d or dc):
+                    go(a2a(u, d, dc))
 
     def link_copy(i, dc, slayer):
         tx = hi * 2 + (lo + i) % 2
@@ -141,8 +134,34 @@
         )
 
     LINKS = [(0, 1), (1, 0), (1, 1)]
-    for i, dc in LINKS:
-        link_copy(i, dc, layer).start()
+
+    def move_links():
+        lcopy.wait()
+        rows = [lbuf[pl.ds(t, 36, stride=8), :] for t in range(8)]
+        link = jnp.concatenate(rows, axis=1)
+        link = jnp.concatenate([link, jnp.zeros((12, 1024), F32)], axis=0)
+        part0 = link.astype(BF16)
+        rest = link - part0.astype(F32)
+        part1 = rest.astype(BF16)
+        part2 = (rest - part1.astype(F32)).astype(BF16)
+        parts = jnp.concatenate([part0, part1, part2], axis=0)
+        for i in range(2):
+            slot = 0 if i == 0 else 1 + 2 * lo
+            got = jnp.dot(parts, perm[slot], preferred_element_type=F32)
+            total = (got[0:48] + got[48:96]) + got[96:144]
+            for dc in (0, 1):
+                piece = total[:, dc * 128:(dc + 1) * 128]
+                if i or dc:
+                    lsend[i * 2 + dc] = piece
+                else:
+                    ul[layer] = piece
+        for i, dc in LINKS:
+            go(link_copy(i, dc, layer))
+
+    move(0)
+    move_links()
+    for u in range(1, NSUB):
+        move(u)
     for i, dc in LINKS:
         link_copy(i, dc, ((lo + i) % 2) * 2 + (c + dc) % 2).wait_recv()
 
@@ -162,16 +181,17 @@
             out.append((are, aim))
         return out
 
-    def put(l, d, v, rows, f):
+    def put(l, d, v, u, r0, f):
         for m in range(2):
             cs = ct[pl.ds(m * 4 + l, 1), :]
             sn = st[pl.ds(m * 4 + l, 1), :]
+            cols = pl.ds(pl.multiple_of(u * 6 * U + (m * 3 + d) * U + r0, 16), 16)
             for r in range(3):
                 fre, fim = f[r]
                 wre = (fre * cs + fim * sn).astype(BF16)
                 wim = (fim * cs - fre * sn).astype(BF16)
-                wt[m * 3 + d, v, rows, pl.ds((l * 6 + r) * 128, 128)] = wre
-                wt[m * 3 + d, v, rows, pl.ds((l * 6 + 3 + r) * 128, 128)] = wim
+                wt[v, cols, pl.ds((l * 6 + r) * 128, 128)] = wre
+                wt[v, cols, pl.ds((l * 6 + 3 + r) * 128, 128)] = wim
 
     def xh_copy(u):
         return remote(
@@ -186,12 +206,9 @@
         )
 
     CH = U // 16
-    for u in range(NSUB):
-        for d, dc in PEERS_X:
-            a2a_in(u, d, dc).wait_recv()
-        xh_copy(u).start()
-
-        def pack(j, carry):
+
+    def pack(u):
+        def body(j, carry):
             rows = pl.ds(pl.multiple_of(u * U + j * 16, 16), 16)
             for i in range(6):
                 acc = lhs[i, 0, rows, :].astype(F32)
@@ -206,29 +223,30 @@
                         neg[l * 3 + r, v, rows, :] = -lhs[l * 6 + 3 + r, v, rows, :]
             return carry
 
-        lax.fori_loop(0, CH, pack, 0)
-        yh_copy(u).start()
-
-        def free(j, carry):
+        lax.fori_loop(0, CH, body, 0)
+
+    def free(u):
+        def body(j, carry):
             v = j // CH
-            rows = pl.ds(pl.multiple_of(u * U + (j % CH) * 16, 16), 16)
+            r0 = (j % CH) * 16
+            rows = pl.ds(pl.multiple_of(u * U + r0, 16), 16)
             for l in range(4):
                 f = [lhs[l * 6 + i, v, rows, :].astype(F32) for i in range(6)]
-                put(l, 0, v, rows, [(f[r], f[3 + r]) for r in range(3)])
+                put(l, 0, v, u, r0, [(f[r], f[3 + r]) for r in range(3)])
                 if l < 3:
                     f = [lhs[l * 6 + 6 + i, v, rows, :].astype(F32) for i in range(6)]
-                    put(l, 1, v, rows, transport(l, 0, f))
+                    put(l, 1, v, u, r0, transport(l, 0, f))
             return carry
 
-        lax.fori_loop(0, 2 * CH, free, 0)
-        xh_copy(u).wait_recv()
-        yh_copy(u).wait_recv()
-
-        def halo(j, carry):
+        lax.fori_loop(0, 2 * CH, body, 0)
+
+    def halo(u):
+        def body(j, carry):
             v = j // CH
-            rows = pl.ds(pl.multiple_of(u * U + (j % CH) * 16, 16), 16)
+            r0 = (j % CH) * 16
+            rows = pl.ds(pl.multiple_of(u * U + r0, 16), 16)
             f = [xh[i, v, rows, :].astype(F32) for i in range(6)]
-            put(3, 1, v, rows, transport(3, 0, f))
+            put(3, 1, v, u, r0, transport(3, 0, f))
             for l in range(4):
                 f = []
                 for i in range(6):
@@ -236,38 +254,82 @@
                     shift = (248 - 8 * (v * 4 + l)) % 128
                     edge = pltpu.roll(hr[i, rows, :].astype(F32), shift, 1)
                     f.append(jnp.where(lane16 < 120, here, edge))
-                put(l, 2, v, rows, transport(l, 1, f))
+                put(l, 2, v, u, r0, transport(l, 1, f))
             return carry
 
-        lax.fori_loop(0, 2 * CH, halo, 0)
-
-    def core_copy(mk):
-        return remote(ex.at[mk], er.at[mk], c_s.at[mk], c_r.at[mk], dev(dc=1))
-
-    def products(mk, carry):
-        right = wt[mk].reshape(256, 3072)
-        re = [lhs[t].reshape(256, 128) for t in range(24)]
+        lax.fori_loop(0, 2 * CH, body, 0)
+
+    def core_copy(j):
+        return remote(ex.at[j], er.at[j], c_s.at[j], c_r.at[j], dev(dc=1))
+
+    def product(j, first, last):
+        count = (last - first) * U
+        sub = slice(first * U, last * U)
+        right = wt[:, pl.ds(pl.multiple_of(j * 128, 128), 128), :].reshape(256, 3072)
+        re = [lhs[t, :, sub, :].reshape(2 * count, 128) for t in range(24)]
         im = []
         for l in range(4):
-            im += [neg[l * 3 + r].reshape(256, 128) for r in range(3)]
-            im += [lhs[l * 6 + r].reshape(256, 128) for r in range(3)]
-        for part, tiles in enumerate((re, im)):
-            left = jnp.concatenate(tiles, axis=1)
-            prod = lax.dot_general(left, right, NT, preferred_element_type=F32)
-            groups = prod.reshape(8, 2, 16, 256)
-            even, odd = groups[:, 0], groups[:, 1]
-            ek[mk, part] = jnp.where(c == 0, even, odd)
-            ex[mk, part] = jnp.where(c == 0, odd, even).astype(BF16)
-        core_copy(mk).start()
-        return carry
-
-    lax.fori_loop(0, 6, products, 0)
+            im += [neg[l * 3 + r, :, sub, :].reshape(2 * count, 128) for r in range(3)]
+            im += [lhs[l * 6 + r, :, sub, :].reshape(2 * count, 128) for r in range(3)]
+        left = jnp.concatenate([jnp.concatenate(re, axis=1), jnp.concatenate(im, axis=1)], axis=0)
+        prod = lax.dot_general(left, right, NT, preferred_element_type=F32)
+        groups = prod.reshape(2, 2, count // 32, 2, 16, 256)
+        for part in range(2):
+            for v in range(2):
+                even, odd = groups[part, v, :, 0], groups[part, v, :, 1]
+                at = slice(v * 4 + first * U // 32, v * 4 + last * U // 32)
+                ek[j, part, at] = jnp.where(c == 0, even, odd)
+                ex[j, part, at] = jnp.where(c == 0, odd, even)
+
+    done = 0
+    done_cols = 0
+
+    def products(upto):
+        nonlocal done, done_cols
+        cols = upto * 6 * U // 128
+        ends = upto == NSUB
+
+        def old(j, carry):
+            product(j, done, upto)
+            if ends:
+                core_copy(j).start()
+            return carry
+
+        def new(j, carry):
+            product(j, 0, upto)
+            if ends:
+                core_copy(j).start()
+            return carry
+
+        if done_cols and upto > done:
+            lax.fori_loop(0, done_cols, old, 0)
+        if cols > done_cols:
+            lax.fori_loop(done_cols, cols, new, 0)
+        done, done_cols = upto, cols
+
+    for u in range(NSUB):
+        for d, dc in PEERS_X:
+            a2a_in(u, d, dc).wait_recv()
+        if u + AHEAD < NSUB:
+            for d, dc in PEERS_X:
+                go(a2a(u + AHEAD, d, dc))
+        go(xh_copy(u))
+        pack(u)
+        go(yh_copy(u))
+        free(u)
+        if u in POINTS:
+            products(u)
+        xh_copy(u).wait_recv()
+        yh_copy(u).wait_recv()
+        halo(u)
+    products(NSUB)
+    pending.extend(core_copy(j) for j in range(6))
 
     for mk in range(6):
         core_copy(mk).wait_recv()
         k = mk % 3
         for part in range(2):
-            total = ek[mk, part] + er[mk, part].astype(F32)
+            total = ek[mk, part] + er[mk, part]
             if mk < 3:
                 ek[mk, part] = total
                 for t in range(4):
@@ -286,8 +348,8 @@
         return remote(sx.at[(x + d) % 4], rx.at[d - 1], x1_s.at[d - 1], x1_r.at[d - 1], dev(dx=d))
 
     for d in (2, 1, 3):
-        z1(d).start()
-        x1(d).start()
+        go(z1(d))
+        go(x1(d))
     for d in (1, 3, 2):
         z1(d).wait_recv()
         x1(d).wait_recv()
@@ -312,8 +374,8 @@
         return remote(sx2.at[(x + d) % 4], rx2.at[d - 1], x2_s.at[d - 1], x2_r.at[d - 1], dev(dx=d))
 
     for d in (2, 1, 3):
-        z2(d).start()
-        x2(d).start()
+        go(z2(d))
+        go(x2(d))
     for d in (1, 3, 2):
         z2(d).wait_recv()
         x2(d).wait_recv()
@@ -333,33 +395,30 @@
         return remote(sy.at[(gy + d) % 4], ry.at[d - 1], y3_s.at[d - 1], y3_r.at[d - 1], dev(dy=d))
 
     for d in (2, 1, 3):
-        y3(d).start()
+        go(y3(d))
     for d in (1, 3, 2):
         y3(d).wait_recv()
     fin[...] = (((sy[gy] + ry[0]) + ry[1]) + ry[2]) * SCALE
+    tiles = [fin[pl.ds(t * 8, 8), :] for t in range(6)]
+    lane8 = lax.broadcasted_iota(jnp.int32, (8, 128), 1)
+
+    def natural(mk):
+        out = None
+        for u in range(NSUB):
+            at = u * 6 * U + mk * U
+            turned = pltpu.roll(tiles[at // 128], (u * U - at) % 128, 1)
+            out = turned if out is None else jnp.where(lane8 < u * U, out, turned)
+        return out
+
     for m in range(2):
-        for part in range(2):
-            by_dir = [fin[pl.ds(((m * 3 + d) * 2 + part) * 4, 4), :] for d in range(3)]
-            for k in range(3):
-                want_dir = dir_ref[k]
-                val = jnp.where(want_dir == 0, by_dir[0], jnp.where(want_dir == 1, by_dir[1], by_dir[2]))
-                out_ref[pl.ds((m * 3 + k) * 2 + part, 4, stride=12), :] = val
-
-    for u in range(NSUB):
-        for d, dc in PEERS_X:
-            a2a(u, d, dc).wait_send()
-        xh_copy(u).wait_send()
-        yh_copy(u).wait_send()
-    for i, dc in LINKS:
-        link_copy(i, dc, layer).wait_send()
-    for mk in range(6):
-        core_copy(mk).wait_send()
-    for d in (1, 2, 3):
-        z1(d).wait_send()
-        x1(d).wait_send()
-        z2(d).wait_send()
-        x2(d).wait_send()
-        y3(d).wait_send()
+        by_dir = [natural(m * 3 + d) for d in range(3)]
+        for k in range(3):
+            want_dir = dir_ref[k]
+            val = jnp.where(want_dir == 0, by_dir[0], jnp.where(want_dir == 1, by_dir[1], by_dir[2]))
+            for part in range(2):
+                out_ref[pl.ds((m * 3 + k) * 2 + part, 4, stride=12), :] = val[part * 4:part * 4 + 4]
+
+    finish()
 
 
 def per_device(vectors, links, momenta, shifts_dir):
@@ -389,16 +448,14 @@
             vm((4, 48, 128), F32),
             vm((8, 128), F32),
             vm((8, 128), F32),
-            vm((6, 2, 128, 3072), BF16),
+            vm((2, 768, 3072), BF16),
             vm((6, 2, 8, 16, 256), F32),
-            vm((6, 2, 8, 16, 256), BF16),
-            vm((6, 2, 8, 16, 256), BF16),
+            vm((6, 2, 8, 16, 256), F32),
+            vm((6, 2, 8, 16, 256), F32),
             vm((4, 3, 2, 2, 16, 256), BF16),
             vm((3, 3, 2, 2, 16, 256), BF16),
             vm((4, 3, 2, 4, 16, 128), BF16),
             vm((3, 3, 2, 4, 16, 128), BF16),
-            vm((8, 128), F32),
-            vm((8, 128), F32),
             vm((4, 3, 2, 16, 128), F32),
             vm((3, 3, 2, 16, 128), F32),
             vm((4, 3, 2, 16, 128), F32),

time: 68.4 us -> 59.6 us (0.87)
  Pallas kernels: 66.8 us -> 58 us
    pallas_call x1, Pallas kernels: 66.8 us -> 58 us  [per_device(): pl.pallas_call(kernel, out_shape=jax.ShapeDtypeStruct((48, 128), F32), in...]
where the time goes in v2:
time: 59.6 us; the launch traced here: 59.4 us
  Pallas kernels  58 us (97%)
  local copies, waits for them, and re-layouts  1.35 us (2%)
    pallas_call x1, Pallas kernels, per_device(): pl.pallas_call(kernel, out_shape=jax.ShapeDtypeStruct((48, 128), F32), in...  58 us
    unnamed x1, local copies, waits for them, and re-layouts  1.35 us

profile of v2, /device:TPU:0, one launch (start us, length us, event | category | flops | bytes accessed | tf_op | source)
XLA Modules:
  0.0 59.4 jit_solution(10416609817459597592)
XLA Ops:
  0.0 58.0 %elementals.1 = f32[48,128]{1,0:T(8,128)} custom-call(bf16[6,128,1024]{2,1,0:T(8,128)(2,1)} %bitcast.3, f32[288,128]{1,0:T(8,128)} %bitcast.4, s32[2,3]{1,0:T(2,128)} %mom_ref.1, s32[3]{0:T(128)} %dir_ref.1), custom_call_target="tpu_custom_call" | custom-call | tf_op jit(solution)/shard_map/elementals/pallas_call | solution.py:427
  58.0 1.4 %copy.6 = f32[4,2,3,2,128]{4,3,2,1,0:T(2,128)} copy(f32[4,2,3,2,128]{4,3,2,1,0:T(2,128)} %bitcast.5) | data formatting | bytes 49152

commit v3 on v2

--- a/solution.py
+++ b/solution.py
@@ -13,7 +13,7 @@
 
 NSUB = 4
 AHEAD = 2
-POINTS = (2, 3)
+SPLIT = True
 U = 128 // NSUB
 NT = (((1,), (1,)), ((), ()))
 SCALE = 1.0 / math.sqrt(3.0 * 16 * 64 * 64)
@@ -23,7 +23,8 @@
 def kernel(
     vec_hbm, links_hbm, mom_ref, dir_ref, out_ref,
     vbuf, lbuf, perm, sbuf, lhs, neg, xh, hs, hr, lsend, ul, ct, st, wt,
-    ek, ex, er, sz, rz, sx, rx, sz2, rz2, sx2, rx2, sy, ry, fin,
+    ek, ex, er, sz_a, rz_a, sx_a, rx_a, sz2_a, rz2_a, sx2_a, rx2_a,
+    sz_b, rz_b, sx_b, rx_b, sz2_b, rz2_b, sx2_b, rx2_b, sy, ry, fin,
     vsem, lsem, a_s, a_r, l_s, l_r, xh_s, xh_r, yh_s, yh_r, c_s, c_r,
     z1_s, z1_r, x1_s, x1_r, z2_s, z2_r, x2_s, x2_r, y3_s, y3_r,
 ):
@@ -281,31 +282,115 @@
                 ek[j, part, at] = jnp.where(c == 0, even, odd)
                 ex[j, part, at] = jnp.where(c == 0, odd, even)
 
-    done = 0
+    done_rows = 0
     done_cols = 0
 
-    def products(upto):
-        nonlocal done, done_cols
-        cols = upto * 6 * U // 128
-        ends = upto == NSUB
+    def products(rows, cols):
+        nonlocal done_rows, done_cols
+        ends = rows == NSUB
+        first = done_rows
 
         def old(j, carry):
-            product(j, done, upto)
+            product(j, first, rows)
             if ends:
                 core_copy(j).start()
             return carry
 
         def new(j, carry):
-            product(j, 0, upto)
+            product(j, 0, rows)
             if ends:
                 core_copy(j).start()
             return carry
 
-        if done_cols and upto > done:
+        if done_cols and rows > done_rows:
             lax.fori_loop(0, done_cols, old, 0)
         if cols > done_cols:
             lax.fori_loop(done_cols, cols, new, 0)
-        done, done_cols = upto, cols
+        done_rows, done_cols = rows, cols
+
+    class Group:
+        def __init__(self, n, jz, jx, refs):
+            self.n, self.jz, self.jx = n, jz, jx
+            (self.sz, self.rz, self.sx, self.rx, self.sz2, self.rz2, self.sx2, self.rx2) = refs
+
+        def z1(self, d):
+            n = self.n
+            return remote(self.sz.at[(z + d) % 4], self.rz.at[d - 1], z1_s.at[n, d - 1], z1_r.at[n, d - 1], dev(dz=d))
+
+        def x1(self, d):
+            n = self.n
+            return remote(self.sx.at[(x + d) % 4], self.rx.at[d - 1], x1_s.at[n, d - 1], x1_r.at[n, d - 1], dev(dx=d))
+
+        def z2(self, d):
+            n = self.n
+            return remote(self.sz2.at[(z + d) % 4], self.rz2.at[d - 1], z2_s.at[n, d - 1], z2_r.at[n, d - 1], dev(dz=d))
+
+        def x2(self, d):
+            n = self.n
+            return remote(self.sx2.at[(x + d) % 4], self.rx2.at[d - 1], x2_s.at[n, d - 1], x2_r.at[n, d - 1], dev(dx=d))
+
+        def first(self):
+            for j in self.jz + self.jx:
+                core_copy(j).wait_recv()
+            for k, j in enumerate(self.jz):
+                for part in range(2):
+                    total = ek[j, part] + er[j, part]
+                    ek[j, part] = total
+                    for t in range(4):
+                        self.sz[t, k, part] = total[2 * t:2 * t + 2].astype(BF16)
+            for d in (2, 1, 3):
+                go(self.z1(d))
+            for k, j in enumerate(self.jx):
+                for part in range(2):
+                    total = ek[j, part] + er[j, part]
+                    ek[j, part] = total
+                    four = total.reshape(4, 2, 16, 256)
+                    for t in range(4):
+                        half = four[:, t % 2][:, :, (t // 2) * 128:(t // 2) * 128 + 128]
+                        self.sx[t, k, part] = half.astype(BF16)
+            for d in (2, 1, 3):
+                go(self.x1(d))
+
+        def second(self):
+            for d in (1, 3, 2):
+                self.z1(d).wait_recv()
+            for k, j in enumerate(self.jz):
+                for part in range(2):
+                    total = ek[j, part, pl.ds(z * 2, 2)]
+                    for d in range(3):
+                        total = total + self.rz[d, k, part].astype(F32)
+                    for t in range(4):
+                        self.sx2[t, k, part] = total[t % 2, :, (t // 2) * 128:(t // 2) * 128 + 128]
+            for d in (2, 1, 3):
+                go(self.x2(d))
+            for d in (1, 3, 2):
+                self.x1(d).wait_recv()
+            for k, j in enumerate(self.jx):
+                for part in range(2):
+                    for t in range(4):
+                        total = ek[j, part, t * 2 + lo, :, pl.ds(pl.multiple_of(hi * 128, 128), 128)]
+                        for d in range(3):
+                            total = total + self.rx[d, k, part, t].astype(F32)
+                        self.sz2[t, k, part] = total
+            for d in (2, 1, 3):
+                go(self.z2(d))
+
+        def third(self):
+            for js, own, sent, got, copy in (
+                (self.jz, x, self.sx2, self.rx2, self.x2), (self.jx, z, self.sz2, self.rz2, self.z2)
+            ):
+                for d in (1, 3, 2):
+                    copy(d).wait_recv()
+                for k, j in enumerate(js):
+                    for part in range(2):
+                        total = sent[own, k, part]
+                        for d in range(3):
+                            total = total + got[d, k, part]
+                        for t in range(4):
+                            sy[t, pl.ds((j * 2 + part) * 4, 4), :] = total[t * 4:t * 4 + 4]
+
+    early = Group(0, (0, 1), (2, 3), (sz_a, rz_a, sx_a, rx_a, sz2_a, rz2_a, sx2_a, rx2_a))
+    late = Group(1, (4,), (5,), (sz_b, rz_b, sx_b, rx_b, sz2_b, rz2_b, sx2_b, rx2_b))
 
     for u in range(NSUB):
         for d, dc in PEERS_X:
@@ -317,79 +402,29 @@
         pack(u)
         go(yh_copy(u))
         free(u)
-        if u in POINTS:
-            products(u)
-        xh_copy(u).wait_recv()
-        yh_copy(u).wait_recv()
-        halo(u)
-    products(NSUB)
+        if u:
+            xh_copy(u - 1).wait_recv()
+            yh_copy(u - 1).wait_recv()
+            halo(u - 1)
+        if u == 2:
+            products(2, 3)
+        if u == 3:
+            products(4, 4)
+    xh_copy(NSUB - 1).wait_recv()
+    yh_copy(NSUB - 1).wait_recv()
+    halo(NSUB - 1)
+    if SPLIT:
+        early.first()
+        products(4, 6)
+    else:
+        products(4, 6)
+        early.first()
+    early.second()
+    late.first()
+    early.third()
+    late.second()
+    late.third()
     pending.extend(core_copy(j) for j in range(6))
-
-    for mk in range(6):
-        core_copy(mk).wait_recv()
-        k = mk % 3
-        for part in range(2):
-            total = ek[mk, part] + er[mk, part]
-            if mk < 3:
-                ek[mk, part] = total
-                for t in range(4):
-                    sz[t, k, part] = total[2 * t:2 * t + 2].astype(BF16)
-            else:
-                ek[mk, part] = total
-                four = total.reshape(4, 2, 16, 256)
-                for t in range(4):
-                    half = four[:, t % 2][:, :, (t // 2) * 128:(t // 2) * 128 + 128]
-                    sx[t, k, part] = half.astype(BF16)
-
-    def z1(d):
-        return remote(sz.at[(z + d) % 4], rz.at[d - 1], z1_s.at[d - 1], z1_r.at[d - 1], dev(dz=d))
-
-    def x1(d):
-        return remote(sx.at[(x + d) % 4], rx.at[d - 1], x1_s.at[d - 1], x1_r.at[d - 1], dev(dx=d))
-
-    for d in (2, 1, 3):
-        go(z1(d))
-        go(x1(d))
-    for d in (1, 3, 2):
-        z1(d).wait_recv()
-        x1(d).wait_recv()
-    for k in range(3):
-        for part in range(2):
-            total = ek[k, part, pl.ds(z * 2, 2)]
-            for d in range(3):
-                total = total + rz[d, k, part].astype(F32)
-            for t in range(4):
-                sx2[t, k, part] = total[t % 2, :, (t // 2) * 128:(t // 2) * 128 + 128]
-            lo_part = [ek[3 + k, part, t * 2 + lo, :, pl.ds(pl.multiple_of(hi * 128, 128), 128)] for t in range(4)]
-            for t in range(4):
-                total = lo_part[t]
-                for d in range(3):
-                    total = total + rx[d, k, part, t].astype(F32)
-                sz2[t, k, part] = total
-
-    def z2(d):
-        return remote(sz2.at[(z + d) % 4], rz2.at[d - 1], z2_s.at[d - 1], z2_r.at[d - 1], dev(dz=d))
-
-    def x2(d):
-        return remote(sx2.at[(x + d) % 4], rx2.at[d - 1], x2_s.at[d - 1], x2_r.at[d - 1], dev(dx=d))
-
-    for d in (2, 1, 3):
-        go(z2(d))
-        go(x2(d))
-    for d in (1, 3, 2):
-        z2(d).wait_recv()
-        x2(d).wait_recv()
-    for k in range(3):
-        for part in range(2):
-            one = sx2[x, k, part]
-            two = sz2[z, k, part]
-            for d in range(3):
-                one = one + rx2[d, k, part]
-                two = two + rz2[d, k, part]
-            for m, total in enumerate((one, two)):
-                j = (m * 3 + k) * 2 + part
-                for t in range(4):
-                    sy[t, pl.ds(j * 4, 4), :] = total[t * 4:t * 4 + 4]
 
     def y3(d):
         return remote(sy.at[(gy + d) % 4], ry.at[d - 1], y3_s.at[d - 1], y3_r.at[d - 1], dev(dy=d))
@@ -419,6 +454,16 @@
                 out_ref[pl.ds((m * 3 + k) * 2 + part, 4, stride=12), :] = val[part * 4:part * 4 + 4]
 
     finish()
+
+
+def group_scratch(n):
+    vm = pltpu.VMEM
+    return [
+        vm((4, n, 2, 2, 16, 256), BF16), vm((3, n, 2, 2, 16, 256), BF16),
+        vm((4, n, 2, 4, 16, 128), BF16), vm((3, n, 2, 4, 16, 128), BF16),
+        vm((4, n, 2, 16, 128), F32), vm((3, n, 2, 16, 128), F32),
+        vm((4, n, 2, 16, 128), F32), vm((3, n, 2, 16, 128), F32),
+    ]
 
 
 def per_device(vectors, links, momenta, shifts_dir):
@@ -452,21 +497,14 @@
             vm((6, 2, 8, 16, 256), F32),
             vm((6, 2, 8, 16, 256), F32),
             vm((6, 2, 8, 16, 256), F32),
-            vm((4, 3, 2, 2, 16, 256), BF16),
-            vm((3, 3, 2, 2, 16, 256), BF16),
-            vm((4, 3, 2, 4, 16, 128), BF16),
-            vm((3, 3, 2, 4, 16, 128), BF16),
-            vm((4, 3, 2, 16, 128), F32),
-            vm((3, 3, 2, 16, 128), F32),
-            vm((4, 3, 2, 16, 128), F32),
-            vm((3, 3, 2, 16, 128), F32),
+            *group_scratch(2), *group_scratch(1),
             vm((4, 48, 128), F32),
             vm((3, 48, 128), F32),
             vm((48, 128), F32),
             dma(NSUB), pltpu.SemaphoreType.DMA,
             dma(NSUB, 8), dma(NSUB, 8), dma(4), dma(4),
             dma(NSUB), dma(NSUB), dma(NSUB), dma(NSUB), dma(6), dma(6),
-            dma(3), dma(3), dma(3), dma(3), dma(3), dma(3), dma(3), dma(3), dma(3), dma(3),
+            *[dma(2, 3) for _ in range(8)], dma(3), dma(3),
         ],
         compiler_params=pltpu.CompilerParams(
             collective_id=0, has_side_effects=True, vmem_limit_bytes=56 * 1024 * 1024

time: 59.6 us -> 55.4 us (0.930)
  Pallas kernels: 58 us -> 53.8 us
    pallas_call x1, Pallas kernels: 58 us -> 53.8 us  [per_device(): pl.pallas_call(kernel, out_shape=jax.ShapeDtypeStruct((48, 128), F32), in...]
where the time goes in v3:
time: 55.4 us; the launch traced here: 55.2 us
  Pallas kernels  53.8 us (97%)
  local copies, waits for them, and re-layouts  1.35 us (2%)
    pallas_call x1, Pallas kernels, per_device(): pl.pallas_call(kernel, out_shape=jax.ShapeDtypeStruct((48, 128), F32), in...  53.8 us
    unnamed x1, local copies, waits for them, and re-layouts  1.35 us

profile of v3, /device:TPU:0, one launch (start us, length us, event | category | flops | bytes accessed | tf_op | source)
XLA Modules:
  0.0 55.2 jit_solution(518051884696889842)
XLA Ops:
  0.0 53.8 %elementals.1 = f32[48,128]{1,0:T(8,128)} custom-call(bf16[6,128,1024]{2,1,0:T(8,128)(2,1)} %bitcast.3, f32[288,128]{1,0:T(8,128)} %bitcast.4, s32[2,3]{1,0:T(2,128)} %mom_ref.1, s32[3]{0:T(128)} %dir_ref.1), custom_call_target="tpu_custom_call" | custom-call | tf_op jit(solution)/shard_map/elementals/pallas_call | solution.py:472
  53.9 1.4 %copy.6 = f32[4,2,3,2,128]{4,3,2,1,0:T(2,128)} copy(f32[4,2,3,2,128]{4,3,2,1,0:T(2,128)} %bitcast.5) | data formatting | bytes 49152

commit v4 on v3

--- a/solution.py
+++ b/solution.py
@@ -13,7 +13,6 @@
 
 NSUB = 4
 AHEAD = 2
-SPLIT = True
 U = 128 // NSUB
 NT = (((1,), (1,)), ((), ()))
 SCALE = 1.0 / math.sqrt(3.0 * 16 * 64 * 64)
@@ -21,8 +20,9 @@
 
 
 def kernel(
-    vec_hbm, links_hbm, mom_ref, dir_ref, out_ref,
-    vbuf, lbuf, perm, sbuf, lhs, neg, xh, hs, hr, lsend, ul, ct, st, wt,
+    vec_hbm, links_hbm, mom_hbm, dir_hbm, out_ref,
+    mom_ref, dir_ref, small_sem,
+    vbuf, lbuf, perm, sbuf, lhs, neg, xh, hs, hr, lsend, ul, ct, st, wt_a, wt_b, wt_c,
     ek, ex, er, sz_a, rz_a, sx_a, rx_a, sz2_a, rz2_a, sx2_a, rx2_a,
     sz_b, rz_b, sx_b, rx_b, sz2_b, rz2_b, sx2_b, rx2_b, sy, ry, fin,
     vsem, lsem, a_s, a_r, l_s, l_r, xh_s, xh_r, yh_s, yh_r, c_s, c_r,
@@ -55,21 +55,27 @@
             src_ref=src, dst_ref=dst, send_sem=s, recv_sem=r, device_id=where, device_id_type=MESH
         )
 
-    loads = []
-    for u in range(NSUB):
-        cp = pltpu.make_async_copy(
-            vec_hbm.at[:, pl.ds(u * U, U), :], vbuf.at[:, pl.ds(u * U, U), :], vsem.at[u]
-        )
-        cp.start()
-        loads.append(cp)
-    lcopy = pltpu.make_async_copy(links_hbm, lbuf, lsem)
-    lcopy.start()
-
     barrier = pltpu.get_barrier_semaphore()
     peers = [dev(dx=d, dc=dc) for d, dc in PEERS_X]
     peers += [dev(dz=d) for d in (1, 2, 3)] + [dev(dy=d) for d in (1, 2, 3)]
     for p in peers:
         pl.semaphore_signal(barrier, inc=1, device_id=p, device_id_type=MESH)
+
+    small = [
+        pltpu.make_async_copy(mom_hbm, mom_ref, small_sem.at[0]),
+        pltpu.make_async_copy(dir_hbm, dir_ref, small_sem.at[1]),
+    ]
+    for cp in small:
+        cp.start()
+    loads = []
+    for u in range(NSUB):
+        cp = pltpu.make_async_copy(
+            vec_hbm.at[:, pl.ds(u * U, U), :], vbuf.at[:, pl.ds(u * U, U), :], vsem.at[u]
+        )
+        cp.start()
+        loads.append(cp)
+    lcopy = pltpu.make_async_copy(links_hbm, lbuf, lsem)
+    lcopy.start()
 
     site = lax.broadcasted_iota(jnp.int32, (1024, 256), 0)
     col = lax.broadcasted_iota(jnp.int32, (1024, 256), 1)
@@ -79,6 +85,9 @@
     for d in range(4):
         q = (x + d) % 4
         perm[d] = jnp.where(site == want + q * 16, 1.0, 0.0).astype(BF16)
+
+    for cp in small:
+        cp.wait()
 
     row = lax.broadcasted_iota(jnp.int32, (8, 128), 0)
     ln = lax.broadcasted_iota(jnp.int32, (8, 128), 1)
@@ -182,11 +191,15 @@
             out.append((are, aim))
         return out
 
+    WT = ((wt_a, 0, 384), (wt_b, 384, 128), (wt_c, 512, 256))
+
     def put(l, d, v, u, r0, f):
         for m in range(2):
             cs = ct[pl.ds(m * 4 + l, 1), :]
             sn = st[pl.ds(m * 4 + l, 1), :]
-            cols = pl.ds(pl.multiple_of(u * 6 * U + (m * 3 + d) * U + r0, 16), 16)
+            at = u * 6 * U + (d * 2 + m) * U
+            wt, base = next((w, b) for w, b, n in WT if b <= at < b + n)
+            cols = pl.ds(pl.multiple_of(at - base + r0, 16), 16)
             for r in range(3):
                 fre, fim = f[r]
                 wre = (fre * cs + fim * sn).astype(BF16)
@@ -226,39 +239,50 @@
 
         lax.fori_loop(0, CH, body, 0)
 
+    def free_chunk(u, j):
+        v = j // CH
+        r0 = (j % CH) * 16
+        rows = pl.ds(pl.multiple_of(u * U + r0, 16), 16)
+        for l in range(4):
+            f = [lhs[l * 6 + i, v, rows, :].astype(F32) for i in range(6)]
+            put(l, 0, v, u, r0, [(f[r], f[3 + r]) for r in range(3)])
+            if l < 3:
+                f = [lhs[l * 6 + 6 + i, v, rows, :].astype(F32) for i in range(6)]
+                put(l, 1, v, u, r0, transport(l, 0, f))
+
     def free(u):
         def body(j, carry):
-            v = j // CH
-            r0 = (j % CH) * 16
-            rows = pl.ds(pl.multiple_of(u * U + r0, 16), 16)
-            for l in range(4):
-                f = [lhs[l * 6 + i, v, rows, :].astype(F32) for i in range(6)]
-                put(l, 0, v, u, r0, [(f[r], f[3 + r]) for r in range(3)])
-                if l < 3:
-                    f = [lhs[l * 6 + 6 + i, v, rows, :].astype(F32) for i in range(6)]
-                    put(l, 1, v, u, r0, transport(l, 0, f))
+            free_chunk(u, j)
             return carry
 
         lax.fori_loop(0, 2 * CH, body, 0)
 
-    def halo(u):
-        def body(j, carry):
-            v = j // CH
-            r0 = (j % CH) * 16
-            rows = pl.ds(pl.multiple_of(u * U + r0, 16), 16)
+    def halo_chunk(u, j):
+        r0 = j * 16
+        rows = pl.ds(pl.multiple_of(u * U + r0, 16), 16)
+        for v in range(2):
             f = [xh[i, v, rows, :].astype(F32) for i in range(6)]
             put(3, 1, v, u, r0, transport(3, 0, f))
             for l in range(4):
                 f = []
                 for i in range(6):
                     here = pltpu.roll(lhs[l * 6 + i, v, rows, :].astype(F32), 120, 1)
-                    shift = (248 - 8 * (v * 4 + l)) % 128
-                    edge = pltpu.roll(hr[i, rows, :].astype(F32), shift, 1)
+                    shift = (120 - 8 * (v * 4 + l)) % 128
+                    edge = hr[i, rows, :].astype(F32)
+                    edge = pltpu.roll(edge, shift, 1) if shift else edge
                     f.append(jnp.where(lane16 < 120, here, edge))
                 put(l, 2, v, u, r0, transport(l, 1, f))
+
+    def halo_wait(u):
+        xh_copy(u).wait_recv()
+        yh_copy(u).wait_recv()
+
+    def halo(u):
+        def body(j, carry):
+            halo_chunk(u, j)
             return carry
 
-        lax.fori_loop(0, 2 * CH, body, 0)
+        lax.fori_loop(0, CH, body, 0)
 
     def core_copy(j):
         return remote(ex.at[j], er.at[j], c_s.at[j], c_r.at[j], dev(dc=1))
@@ -266,7 +290,11 @@
     def product(j, first, last):
         count = (last - first) * U
         sub = slice(first * U, last * U)
-        right = wt[:, pl.ds(pl.multiple_of(j * 128, 128), 128), :].reshape(256, 3072)
+        if isinstance(j, int) and j >= 3:
+            wt, base, _ = WT[1 if j == 3 else 2]
+            right = wt[:, j * 128 - base:j * 128 - base + 128, :].reshape(256, 3072)
+        else:
+            right = wt_a[:, pl.ds(pl.multiple_of(j * 128, 128), 128), :].reshape(256, 3072)
         re = [lhs[t, :, sub, :].reshape(2 * count, 128) for t in range(24)]
         im = []
         for l in range(4):
@@ -282,32 +310,6 @@
                 ek[j, part, at] = jnp.where(c == 0, even, odd)
                 ex[j, part, at] = jnp.where(c == 0, odd, even)
 
-    done_rows = 0
-    done_cols = 0
-
-    def products(rows, cols):
-        nonlocal done_rows, done_cols
-        ends = rows == NSUB
-        first = done_rows
-
-        def old(j, carry):
-            product(j, first, rows)
-            if ends:
-                core_copy(j).start()
-            return carry
-
-        def new(j, carry):
-            product(j, 0, rows)
-            if ends:
-                core_copy(j).start()
-            return carry
-
-        if done_cols and rows > done_rows:
-            lax.fori_loop(0, done_cols, old, 0)
-        if cols > done_cols:
-            lax.fori_loop(done_cols, cols, new, 0)
-        done_rows, done_cols = rows, cols
-
     class Group:
         def __init__(self, n, jz, jx, refs):
             self.n, self.jz, self.jx = n, jz, jx
@@ -330,48 +332,44 @@
             return remote(self.sx2.at[(x + d) % 4], self.rx2.at[d - 1], x2_s.at[n, d - 1], x2_r.at[n, d - 1], dev(dx=d))
 
         def first(self):
-            for j in self.jz + self.jx:
+            for j in sorted({j for j, _ in self.jz + self.jx}):
                 core_copy(j).wait_recv()
-            for k, j in enumerate(self.jz):
-                for part in range(2):
-                    total = ek[j, part] + er[j, part]
-                    ek[j, part] = total
-                    for t in range(4):
-                        self.sz[t, k, part] = total[2 * t:2 * t + 2].astype(BF16)
+            for k, (j, part) in enumerate(self.jz):
+                total = ek[j, part] + er[j, part]
+                ek[j, part] = total
+                for t in range(4):
+                    self.sz[t, k] = total[2 * t:2 * t + 2].astype(BF16)
             for d in (2, 1, 3):
                 go(self.z1(d))
-            for k, j in enumerate(self.jx):
-                for part in range(2):
-                    total = ek[j, part] + er[j, part]
-                    ek[j, part] = total
-                    four = total.reshape(4, 2, 16, 256)
-                    for t in range(4):
-                        half = four[:, t % 2][:, :, (t // 2) * 128:(t // 2) * 128 + 128]
-                        self.sx[t, k, part] = half.astype(BF16)
+            for k, (j, part) in enumerate(self.jx):
+                total = ek[j, part] + er[j, part]
+                ek[j, part] = total
+                four = total.reshape(4, 2, 16, 256)
+                for t in range(4):
+                    half = four[:, t % 2][:, :, (t // 2) * 128:(t // 2) * 128 + 128]
+                    self.sx[t, k] = half.astype(BF16)
             for d in (2, 1, 3):
                 go(self.x1(d))
 
         def second(self):
             for d in (1, 3, 2):
                 self.z1(d).wait_recv()
-            for k, j in enumerate(self.jz):
-                for part in range(2):
-                    total = ek[j, part, pl.ds(z * 2, 2)]
-                    for d in range(3):
-                        total = total + self.rz[d, k, part].astype(F32)
-                    for t in range(4):
-                        self.sx2[t, k, part] = total[t % 2, :, (t // 2) * 128:(t // 2) * 128 + 128]
+            for k, (j, part) in enumerate(self.jz):
+                total = ek[j, part, pl.ds(z * 2, 2)]
+                for d in range(3):
+                    total = total + self.rz[d, k].astype(F32)
+                for t in range(4):
+                    self.sx2[t, k] = total[t % 2, :, (t // 2) * 128:(t // 2) * 128 + 128]
             for d in (2, 1, 3):
                 go(self.x2(d))
             for d in (1, 3, 2):
                 self.x1(d).wait_recv()
-            for k, j in enumerate(self.jx):
-                for part in range(2):
-                    for t in range(4):
-                        total = ek[j, part, t * 2 + lo, :, pl.ds(pl.multiple_of(hi * 128, 128), 128)]
-                        for d in range(3):
-                            total = total + self.rx[d, k, part, t].astype(F32)
-                        self.sz2[t, k, part] = total
+            for k, (j, part) in enumerate(self.jx):
+                for t in range(4):
+                    total = ek[j, part, t * 2 + lo, :, pl.ds(pl.multiple_of(hi * 128, 128), 128)]
+                    for d in range(3):
+                        total = total + self.rx[d, k, t].astype(F32)
+                    self.sz2[t, k] = total
             for d in (2, 1, 3):
                 go(self.z2(d))
 
@@ -381,48 +379,67 @@
             ):
                 for d in (1, 3, 2):
                     copy(d).wait_recv()
-                for k, j in enumerate(js):
-                    for part in range(2):
-                        total = sent[own, k, part]
-                        for d in range(3):
-                            total = total + got[d, k, part]
-                        for t in range(4):
-                            sy[t, pl.ds((j * 2 + part) * 4, 4), :] = total[t * 4:t * 4 + 4]
-
-    early = Group(0, (0, 1), (2, 3), (sz_a, rz_a, sx_a, rx_a, sz2_a, rz2_a, sx2_a, rx2_a))
-    late = Group(1, (4,), (5,), (sz_b, rz_b, sx_b, rx_b, sz2_b, rz2_b, sx2_b, rx2_b))
+                for k, (j, part) in enumerate(js):
+                    total = sent[own, k]
+                    for d in range(3):
+                        total = total + got[d, k]
+                    for t in range(4):
+                        sy[t, pl.ds((j * 2 + part) * 4, 4), :] = total[t * 4:t * 4 + 4]
+
+    early = Group(
+        0, ((0, 0), (0, 1), (1, 0), (1, 1)), ((2, 0), (2, 1), (3, 0), (3, 1)),
+        (sz_a, rz_a, sx_a, rx_a, sz2_a, rz2_a, sx2_a, rx2_a),
+    )
+    late = Group(1, ((4, 0), (4, 1)), ((5, 0), (5, 1)), (sz_b, rz_b, sx_b, rx_b, sz2_b, rz2_b, sx2_b, rx2_b))
 
     for u in range(NSUB):
         for d, dc in PEERS_X:
             a2a_in(u, d, dc).wait_recv()
+        go(xh_copy(u))
+        pack(u)
+        go(yh_copy(u))
         if u + AHEAD < NSUB:
             for d, dc in PEERS_X:
                 go(a2a(u + AHEAD, d, dc))
-        go(xh_copy(u))
-        pack(u)
-        go(yh_copy(u))
-        free(u)
-        if u:
-            xh_copy(u - 1).wait_recv()
-            yh_copy(u - 1).wait_recv()
-            halo(u - 1)
-        if u == 2:
-            products(2, 3)
-        if u == 3:
-            products(4, 4)
-    xh_copy(NSUB - 1).wait_recv()
-    yh_copy(NSUB - 1).wait_recv()
-    halo(NSUB - 1)
-    if SPLIT:
-        early.first()
-        products(4, 6)
-    else:
-        products(4, 6)
-        early.first()
+        if u < 3:
+            free(u)
+            if u:
+                halo_wait(u - 1)
+                halo(u - 1)
+            if u == 2:
+                def block(j, carry):
+                    product(j, 0, 2)
+                    return carry
+
+                lax.fori_loop(0, 3, block, 0)
+        else:
+            halo_wait(2)
+
+            def both(j, carry):
+                product(j, 2, 4)
+                halo_chunk(2, j)
+                free_chunk(3, j)
+                core_copy(j).start()
+                return carry
+
+            lax.fori_loop(0, 2, both, 0)
+            product(2, 2, 4)
+            free_chunk(3, 2)
+            core_copy(2).start()
+            product(3, 0, 4)
+            free_chunk(3, 3)
+            core_copy(3).start()
+            product(4, 0, 4)
+            core_copy(4).start()
+            halo_wait(3)
+            halo(3)
+    early.first()
+    product(5, 0, 4)
+    core_copy(5).start()
+    late.first()
     early.second()
-    late.first()
+    late.second()
     early.third()
-    late.second()
     late.third()
     pending.extend(core_copy(j) for j in range(6))
 
@@ -437,16 +454,16 @@
     tiles = [fin[pl.ds(t * 8, 8), :] for t in range(6)]
     lane8 = lax.broadcasted_iota(jnp.int32, (8, 128), 1)
 
-    def natural(mk):
+    def natural(m, d):
         out = None
         for u in range(NSUB):
-            at = u * 6 * U + mk * U
+            at = u * 6 * U + (d * 2 + m) * U
             turned = pltpu.roll(tiles[at // 128], (u * U - at) % 128, 1)
             out = turned if out is None else jnp.where(lane8 < u * U, out, turned)
         return out
 
     for m in range(2):
-        by_dir = [natural(m * 3 + d) for d in range(3)]
+        by_dir = [natural(m, d) for d in range(3)]
         for k in range(3):
             want_dir = dir_ref[k]
             val = jnp.where(want_dir == 0, by_dir[0], jnp.where(want_dir == 1, by_dir[1], by_dir[2]))
@@ -459,10 +476,10 @@
 def group_scratch(n):
     vm = pltpu.VMEM
     return [
-        vm((4, n, 2, 2, 16, 256), BF16), vm((3, n, 2, 2, 16, 256), BF16),
-        vm((4, n, 2, 4, 16, 128), BF16), vm((3, n, 2, 4, 16, 128), BF16),
-        vm((4, n, 2, 16, 128), F32), vm((3, n, 2, 16, 128), F32),
-        vm((4, n, 2, 16, 128), F32), vm((3, n, 2, 16, 128), F32),
+        vm((4, n, 2, 16, 256), BF16), vm((3, n, 2, 16, 256), BF16),
+        vm((4, n, 4, 16, 128), BF16), vm((3, n, 4, 16, 128), BF16),
+        vm((4, n, 16, 128), F32), vm((3, n, 16, 128), F32),
+        vm((4, n, 16, 128), F32), vm((3, n, 16, 128), F32),
     ]
 
 
@@ -475,11 +492,12 @@
         in_specs=[
             pl.BlockSpec(memory_space=pl.ANY),
             pl.BlockSpec(memory_space=pl.ANY),
-            pl.BlockSpec(memory_space=pltpu.SMEM),
-            pl.BlockSpec(memory_space=pltpu.SMEM),
+            pl.BlockSpec(memory_space=pl.ANY),
+            pl.BlockSpec(memory_space=pl.ANY),
         ],
         out_specs=pl.BlockSpec(memory_space=pltpu.VMEM),
         scratch_shapes=[
+            pltpu.SMEM((2, 3), jnp.int32), pltpu.SMEM((3,), jnp.int32), dma(2),
             vm((6, 128, 1024), BF16),
             vm((288, 128), F32),
             vm((4, 1024, 256), BF16),
@@ -493,11 +511,13 @@
             vm((4, 48, 128), F32),
             vm((8, 128), F32),
             vm((8, 128), F32),
-            vm((2, 768, 3072), BF16),
+            vm((2, 384, 3072), BF16),
+            vm((2, 128, 3072), BF16),
+            vm((2, 256, 3072), BF16),
             vm((6, 2, 8, 16, 256), F32),
             vm((6, 2, 8, 16, 256), F32),
             vm((6, 2, 8, 16, 256), F32),
-            *group_scratch(2), *group_scratch(1),
+            *group_scratch(4), *group_scratch(2),
             vm((4, 48, 128), F32),
             vm((3, 48, 128), F32),
             vm((48, 128), F32),

time: 55.4 us -> 52.8 us (0.953)
  Pallas kernels: 53.8 us -> 51.3 us
    pallas_call x1, Pallas kernels: 53.8 us -> 51.3 us  [per_device(): pl.pallas_call(kernel, out_shape=jax.ShapeDtypeStruct((48, 128), F32), in...]
where the time goes in v4:
time: 52.8 us; the launch traced here: 52.7 us
  Pallas kernels  51.3 us (97%)
  local copies, waits for them, and re-layouts  1.35 us (3%)
    pallas_call x1, Pallas kernels, per_device(): pl.pallas_call(kernel, out_shape=jax.ShapeDtypeStruct((48, 128), F32), in...  51.3 us
    unnamed x1, local copies, waits for them, and re-layouts  1.35 us

profile of v4, /device:TPU:0, one launch (start us, length us, event | category | flops | bytes accessed | tf_op | source)
XLA Modules:
  0.0 52.7 jit_solution(6410459946716266491)
XLA Ops:
  0.0 51.3 %elementals.1 = f32[48,128]{1,0:T(8,128)} custom-call(bf16[6,128,1024]{2,1,0:T(8,128)(2,1)} %bitcast.3, f32[288,128]{1,0:T(8,128)} %bitcast.4, s32[2,3]{1,0:T(2,128)} %mom_hbm.1, s32[3]{0:T(128)} %dir_hbm.1), custom_call_target="tpu_custom_call" | custom-call | tf_op jit(solution)/shard_map/elementals/pallas_call | solution.py:489
  51.3 1.4 %copy.6 = f32[4,2,3,2,128]{4,3,2,1,0:T(2,128)} copy(f32[4,2,3,2,128]{4,3,2,1,0:T(2,128)} %bitcast.5) | data formatting | bytes 49152
